TPU v7x, 32 devices: a whole 2x2x4 slice. The times are simulated.
32 devices in a mesh: tok: 8 (over y, x, core), feat: 4 (over z).
Axes of the slice: x: 2, y: 2, z: 4, core: 2. Of those that a mesh axis runs over, the one named last changes fastest.
Arguments:
- resid: bfloat16 [1024, 4096], P('tok'), may hold values from -6 to 6
- enc_weight: bfloat16 [4096, 32768], P(None, ('tok', 'feat')), may hold values from -0.09375 to 0.09375
- enc_bias: float32 [32768], P(('tok', 'feat')), may hold values from -3 to 3
- dec_weight: bfloat16 [32768, 4096], P(('tok', 'feat')), may hold values from -0.0546875 to 0.0546875
- dec_bias: float32 [4096], replicated, may hold values from -3 to 3
- active_ids: int32 [8, 96], replicated, may hold values from 0 to 255, all different within a row; in each aligned block of 8 rows (0 to 7, 8 to 15, ...) at most 4 rows name the same one
Outputs:
- recon_error: float32 [1024, 4096], P('tok', 'feat')
Inputs may be any that keep to these rules, and one draw needn't show every extreme that they name: `active_ids`: the ids of one row block are distinct; each feature block is active in at least one and at most 4 row blocks, and some feature block in exactly 4.
All inputs are finite; a program needn't handle non-finite values.
Results may differ from a plain program's by a relative error of at most 0.009.
Values may be sent and summed in bfloat16 or wider, within the bound.
A program may use at most 192 MiB of HBM per device.

v0:
```python
import jax
import jax.numpy as jnp
from jax import lax
from jax.sharding import PartitionSpec as P

BLK = 128
BLK_DEV = 8


def local(resid, enc_weight, enc_bias, dec_weight, dec_bias, active_ids):
    tok_rows, width = resid.shape
    centered = (resid.astype(jnp.float32) - dec_bias[None, :]).astype(jnp.bfloat16)
    gathered = lax.all_gather(centered, "tok", axis=0, tiled=True)
    row_blocks = gathered.shape[0] // BLK
    tiles = gathered.reshape(row_blocks, BLK, width)
    all_blocks = BLK_DEV * lax.axis_size("tok") * lax.axis_size("feat")
    slot_count = (row_blocks * active_ids.shape[1] + all_blocks - 1) // all_blocks + 1
    device = lax.axis_index("tok") * lax.axis_size("feat") + lax.axis_index("feat")
    owned = device * BLK_DEV + jnp.arange(BLK_DEV, dtype=jnp.int32)
    hits = jnp.any(active_ids[:, :, None] == owned[None, None, :], axis=1)
    ranks = jnp.cumsum(hits.astype(jnp.int32), axis=0) - 1
    slot_range = jnp.arange(slot_count, dtype=jnp.int32)
    match = (hits[:, :, None] & (ranks[:, :, None] == slot_range[None, None, :])).astype(
        jnp.float32
    )
    slot_live = jnp.sum(match, axis=0)

    def one_block(index, partial_value):
        select = lax.dynamic_index_in_dim(match, index, 1, keepdims=False)
        picked = jnp.einsum(
            "rs,rbd->sbd", select.astype(jnp.bfloat16), tiles, preferred_element_type=jnp.float32
        )
        picked = picked.astype(jnp.bfloat16).reshape(slot_count * BLK, width)
        w_in = lax.dynamic_slice_in_dim(enc_weight, index * BLK, BLK, 1)
        bias_in = lax.dynamic_slice_in_dim(enc_bias, index * BLK, BLK, 0)
        pre = jnp.dot(picked, w_in, preferred_element_type=jnp.float32) + bias_in[None, :]
        live = slot_live[index]
        codes = (jnp.maximum(pre, 0.0).reshape(slot_count, BLK, BLK) * live[:, None, None]).astype(
            jnp.bfloat16
        )
        w_out = lax.dynamic_slice_in_dim(dec_weight, index * BLK, BLK, 0)
        contrib = jnp.dot(
            codes.reshape(slot_count * BLK, BLK), w_out, preferred_element_type=jnp.float32
        )
        placed = jnp.einsum(
            "rs,sbd->rbd",
            select,
            contrib.reshape(slot_count, BLK, width),
            precision=lax.Precision.HIGHEST,
        )
        return partial_value + placed

    partial_value = lax.fori_loop(
        0, BLK_DEV, one_block, jnp.zeros((row_blocks, BLK, width), jnp.float32)
    )
    rounded = lax.optimization_barrier(partial_value.astype(jnp.bfloat16)).astype(jnp.float32)
    rounded = rounded.reshape(row_blocks * BLK, width)
    section_one = lax.psum_scatter(
        rounded.astype(jnp.bfloat16), "feat", scatter_dimension=1, tiled=True
    )
    total = lax.psum_scatter(section_one, "tok", scatter_dimension=0, tiled=True).astype(
        jnp.float32
    )
    columns = total.shape[1]
    start = lax.axis_index("feat") * columns
    bias_part = lax.dynamic_slice_in_dim(dec_bias, start, columns, 0)
    resid_part = lax.dynamic_slice_in_dim(resid, start, columns, 1).astype(jnp.float32)
    return total + bias_part[None, :] - resid_part


def solution(mesh):
    in_specs = (
        P("tok", None),
        P(None, ("tok", "feat")),
        P(("tok", "feat")),
        P(("tok", "feat"), None),
        P(),
        P(),
    )
    out_specs = P("tok", "feat")
    return jax.shard_map(local, mesh=mesh, in_specs=in_specs, out_specs=out_specs, check_vma=False)
```

profile of v0, /device:TPU:0, one launch (start us, length us, event | category | flops | bytes accessed | tf_op | source)
XLA Modules:
  0.0 667.8 jit_solution(1365456165813265296)
XLA Ops:
  10.3 56.0 %all-gather.2.cloned.1.call-done = bf16[1024,4096]{1,0:T(8,128)(2,1)} async-done(((bf16[128,4096]{1,0:T(8,128)(2,1)}), bf16[1024,4096]{1,0:T(8,128)(2,1)}) %all-gather.2.cloned.1.call-update) | async-done | bytes 8388624 | tf_op jit(solution)/shard_map/all_gather | solution.py:13
  66.4 11.2 %copy.15 = bf16[8,128,4096]{2,0,1:T(8,128)(2,1)} copy(bf16[8,128,4096]{2,1,0:T(8,128)(2,1)} %bitcast.51) | data formatting | bytes 16777216
  77.6 371.7 %while.14 = (s32[]{:T(128)}, f32[8,128,4096]{2,0,1:T(8,128)}, f32[8,8,4]{0,2,1:T(4,128)S(1)}, bf16[8,128,4096]{2,0,1:T(8,128)(2,1)}, bf16[4096,1024]{1,0:T(8,128...) while((s32[]{:T(128)}, f32[8,128,4096]{2,0,1:T(8,128)}, ...), condition=%wide.region_4.5_spmd.clone, body=%wide.region_3.4_spmd.clone.sunk | while | flops 1319370752 | bytes 77865712 | solution.py:53
  78.3 5.7 convolution_convert_fusion.2
  88.9 5.7 fusion.47
  94.6 28.3 %select_add_fusion.2 = f32[8,128,4096]{2,0,1:T(8,128)} fusion(f32[8,128,4096]{2,0,1:T(8,128)} %get-tuple-element.266, f32[4,128,4096]{2,1,0:T(8,128)} %fusion.47, pred[]{:T(512)S(6)} %compare.3, f32[8,8,4]{0,2,1:T(4,128)S(1)} %get-tuple-element.279, s32[]{:T(128)} %get-tuple-element.265), kind=kOutput, calls=%fused_computation.clone.2 | convolution fusion | flops 209715200 | bytes 41945092 | tf_op jit(solution)/shard_map/while/body/eval_jaxpr/rs,sbd->rbd/dot_general | solution.py:45
  123.7 5.7 convolution_convert_fusion.2
  140.0 29.5 %select_add_fusion.2 = f32[8,128,4096]{2,0,1:T(8,128)} fusion(f32[8,128,4096]{2,0,1:T(8,128)} %get-tuple-element.266, f32[4,128,4096]{2,1,0:T(8,128)} %fusion.47, pred[]{:T(512)S(6)} %compare.3, f32[8,8,4]{0,2,1:T(4,128)S(1)} %get-tuple-element.279, s32[]{:T(128)} %get-tuple-element.265), kind=kOutput, calls=%fused_computation.clone.2 | convolution fusion | flops 209715200 | bytes 41945092 | tf_op jit(solution)/shard_map/while/body/eval_jaxpr/rs,sbd->rbd/dot_general | solution.py:45
  170.3 5.7 convolution_convert_fusion.2
  186.6 29.5 %select_add_fusion.2 = f32[8,128,4096]{2,0,1:T(8,128)} fusion(f32[8,128,4096]{2,0,1:T(8,128)} %get-tuple-element.266, f32[4,128,4096]{2,1,0:T(8,128)} %fusion.47, pred[]{:T(512)S(6)} %compare.3, f32[8,8,4]{0,2,1:T(4,128)S(1)} %get-tuple-element.279, s32[]{:T(128)} %get-tuple-element.265), kind=kOutput, calls=%fused_computation.clone.2 | convolution fusion | flops 209715200 | bytes 41945092 | tf_op jit(solution)/shard_map/while/body/eval_jaxpr/rs,sbd->rbd/dot_general | solution.py:45
  216.9 5.7 convolution_convert_fusion.2
  233.2 29.5 %select_add_fusion.2 = f32[8,128,4096]{2,0,1:T(8,128)} fusion(f32[8,128,4096]{2,0,1:T(8,128)} %get-tuple-element.266, f32[4,128,4096]{2,1,0:T(8,128)} %fusion.47, pred[]{:T(512)S(6)} %compare.3, f32[8,8,4]{0,2,1:T(4,128)S(1)} %get-tuple-element.279, s32[]{:T(128)} %get-tuple-element.265), kind=kOutput, calls=%fused_computation.clone.2 | convolution fusion | flops 209715200 | bytes 41945092 | tf_op jit(solution)/shard_map/while/body/eval_jaxpr/rs,sbd->rbd/dot_general | solution.py:45
  263.5 5.7 convolution_convert_fusion.2
  279.9 29.5 %select_add_fusion.2 = f32[8,128,4096]{2,0,1:T(8,128)} fusion(f32[8,128,4096]{2,0,1:T(8,128)} %get-tuple-element.266, f32[4,128,4096]{2,1,0:T(8,128)} %fusion.47, pred[]{:T(512)S(6)} %compare.3, f32[8,8,4]{0,2,1:T(4,128)S(1)} %get-tuple-element.279, s32[]{:T(128)} %get-tuple-element.265), kind=kOutput, calls=%fused_computation.clone.2 | convolution fusion | flops 209715200 | bytes 41945092 | tf_op jit(solution)/shard_map/while/body/eval_jaxpr/rs,sbd->rbd/dot_general | solution.py:45
  310.2 5.7 convolution_convert_fusion.2
  326.5 29.5 %select_add_fusion.2 = f32[8,128,4096]{2,0,1:T(8,128)} fusion(f32[8,128,4096]{2,0,1:T(8,128)} %get-tuple-element.266, f32[4,128,4096]{2,1,0:T(8,128)} %fusion.47, pred[]{:T(512)S(6)} %compare.3, f32[8,8,4]{0,2,1:T(4,128)S(1)} %get-tuple-element.279, s32[]{:T(128)} %get-tuple-element.265), kind=kOutput, calls=%fused_computation.clone.2 | convolution fusion | flops 209715200 | bytes 41945092 | tf_op jit(solution)/shard_map/while/body/eval_jaxpr/rs,sbd->rbd/dot_general | solution.py:45
  356.8 5.7 convolution_convert_fusion.2
  373.1 29.5 %select_add_fusion.2 = f32[8,128,4096]{2,0,1:T(8,128)} fusion(f32[8,128,4096]{2,0,1:T(8,128)} %get-tuple-element.266, f32[4,128,4096]{2,1,0:T(8,128)} %fusion.47, pred[]{:T(512)S(6)} %compare.3, f32[8,8,4]{0,2,1:T(4,128)S(1)} %get-tuple-element.279, s32[]{:T(128)} %get-tuple-element.265), kind=kOutput, calls=%fused_computation.clone.2 | convolution fusion | flops 209715200 | bytes 41945092 | tf_op jit(solution)/shard_map/while/body/eval_jaxpr/rs,sbd->rbd/dot_general | solution.py:45
  403.4 5.7 convolution_convert_fusion.2
  419.7 29.5 %select_add_fusion.2 = f32[8,128,4096]{2,0,1:T(8,128)} fusion(f32[8,128,4096]{2,0,1:T(8,128)} %get-tuple-element.266, f32[4,128,4096]{2,1,0:T(8,128)} %fusion.47, pred[]{:T(512)S(6)} %compare.3, f32[8,8,4]{0,2,1:T(4,128)S(1)} %get-tuple-element.279, s32[]{:T(128)} %get-tuple-element.265), kind=kOutput, calls=%fused_computation.clone.2 | convolution fusion | flops 209715200 | bytes 41945092 | tf_op jit(solution)/shard_map/while/body/eval_jaxpr/rs,sbd->rbd/dot_general | solution.py:45
  449.2 9.0 %convert_element_type.56 = bf16[8,128,4096]{2,0,1:T(8,128)(2,1)} convert(f32[8,128,4096]{2,0,1:T(8,128)} %get-tuple-element.144) | non-fusion elementwise | flops 4194304 | bytes 25165824 | tf_op jit(solution)/shard_map/convert_element_type | solution.py:56
  458.3 11.2 %copy.16 = bf16[8,128,4096]{2,1,0:T(8,128)(2,1)} copy(bf16[8,128,4096]{2,0,1:T(8,128)(2,1)} %convert_element_type.56) | data formatting | bytes 16777216 | tf_op jit(solution)/shard_map/optimization_barrier | solution.py:56
  469.5 144.6 %reduce-scatter.3.cloned.1.call-done = bf16[1024,1024]{1,0:T(8,128)(2,1)} async-done(((bf16[1024,4096]{1,0:T(8,128)(2,1)}), bf16[1024,1024]{1,0:T(8,128)(2,1)}) %reduce-scatter.3.cloned.1.call-update) | async-done | bytes 2097168 | tf_op jit(solution)/shard_map/reduce_scatter | solution.py:58
  614.8 44.5 %reduce-scatter.5.cloned.1.call-done = bf16[128,1024]{1,0:T(8,128)(2,1)} async-done(((bf16[1024,1024]{1,0:T(8,128)(2,1)}), bf16[128,1024]{1,0:T(8,128)(2,1)}) %reduce-scatter.5.cloned.1.call-update) | async-done | bytes 262160 | tf_op jit(solution)/shard_map/reduce_scatter | solution.py:61
  (66 shorter events, 91.5 us)
Async XLA Ops:
  6.5 59.8 %all-gather.2.cloned.1.call-start = ((), (), s32[]{:S(2)}) async-start(), calls=%async_computation.2 | async-start | bytes 9437184 | tf_op jit(solution)/shard_map/all_gather | solution.py:13
  9.0 605.1 %reduce-scatter.3.cloned.1.call-start = ((), (), s32[]{:S(2)}) async-start(), calls=%async_computation.3 | async-start | bytes 10485760 | tf_op jit(solution)/shard_map/reduce_scatter | solution.py:58
  469.5 189.9 %reduce-scatter.5.cloned.1.call-start = ((), (), s32[]{:S(2)}) async-start(), calls=%async_computation.4 | async-start | bytes 2359296 | tf_op jit(solution)/shard_map/reduce_scatter | solution.py:61
Sparse Core Ops, SparseCore 0:
  9.2 57.0 all-gather.1
  469.6 144.4 reduce-scatter.2
  617.4 41.9 reduce-scatter.4
where the time goes:
time: 669 us; the launch traced here: 668 us
  matrix products  346 us (52%)
  waiting for transfers between devices  245 us (37%)
  local copies, waits for them, and re-layouts  48.4 us (7%)
  other arithmetic  14.4 us (2%)
  between operations  13.1 us (2%)
    dot_general x8, matrix products, one_block(): jnp.einsum('rs,sbd->rbd', select, contrib.reshape(slot_count, BLK, width)...  235 us
    reduce_scatter x1, waiting for transfers between devices, local(): lax.psum_scatter(rounded.astype(jnp.bfloat16), 'feat', scatter_dimension=...  145 us
    all_gather x1, waiting for transfers between devices, local(): gathered = lax.all_gather(centered, 'tok', axis=0, tiled=True)  56 us
    dot_general x8, matrix products, one_block(): jnp.einsum('rs,rbd->sbd', select.astype(jnp.bfloat16), tiles, preferred_e...  45.6 us
    dot_general x8, matrix products, one_block(): jnp.dot(codes.reshape(slot_count * BLK, BLK), w_out, preferred_element_ty...  45.5 us
    reduce_scatter x1, waiting for transfers between devices, local(): lax.psum_scatter(section_one, 'tok', scatter_dimension=0, tiled=True)  44.5 us
    dot_general x8, matrix products, one_block(): jnp.dot(picked, w_in, preferred_element_type=jnp.float32) + bias_in[None, :]  20.2 us
    convert_element_type x8, local copies, waits for them, and re-layouts, one_block(): picked = picked.astype(jnp.bfloat16).reshape(slot_count * BLK, width)  18.4 us
  transfers between devices with their start and end apart: 3, of which 3 were waited for; matrix products, arithmetic and copies ran while one was open for 0% of the time, Pallas kernels for 0%

commit v1 on v0

--- a/solution.py
+++ b/solution.py
@@ -1,10 +1,14 @@
 import jax
 import jax.numpy as jnp
 from jax import lax
+from jax.experimental import pallas as pl
+from jax.experimental.pallas import tpu as pltpu
 from jax.sharding import PartitionSpec as P
 
 BLK = 128
 BLK_DEV = 8
+CHUNKS = 4
+MESH = pl.DeviceIdType.MESH
 
 
 def local(resid, enc_weight, enc_bias, dec_weight, dec_bias, active_ids):
@@ -68,6 +72,258 @@
     return total + bias_part[None, :] - resid_part
 
 
+def fused(resid_ref, enc_ref, ebias_ref, dec_ref, dbias_ref, ids_ref, out_ref,
+          xs, enc_v, dec_v, codes, part, from_core, from_first, from_second, from_z, active,
+          load_sem, ag_send, ag_recv, core_send, core_recv, first_send, first_recv,
+          second_send, second_recv, z_send, z_recv):
+    t = lax.axis_index("tok")
+    z = lax.axis_index("feat")
+    n_z = lax.axis_size("feat")
+    core = lax.rem(t, 2)
+    chip = t // 2
+    x = lax.rem(chip, 2)
+    y = chip // 2
+    chips = 4
+    mine, other = core * chips, (1 - core) * chips
+    chip_x, chip_y, chip_d = y * 2 + 1 - x, (1 - y) * 2 + x, (1 - y) * 2 + 1 - x
+    sibling = (chip * 2 + 1 - core, z)
+    by_x = (chip_x * 2 + core, z)
+    by_y = (chip_y * 2 + core, z)
+    along_z = [(t, lax.rem(z + d, n_z)) for d in range(1, n_z)]
+    width = resid_ref.shape[1]
+    own = width // n_z
+    step = own // CHUNKS
+    half = BLK // 2
+
+    load_enc = pltpu.make_async_copy(enc_ref, enc_v, load_sem.at[0])
+    load_dec = pltpu.make_async_copy(dec_ref, dec_v, load_sem.at[1])
+    load_enc.start()
+    load_dec.start()
+
+    barrier = pltpu.get_barrier_semaphore()
+    greeted = [sibling, by_x, by_y] + along_z
+    for who in greeted:
+        pl.semaphore_signal(barrier, inc=1, device_id=who, device_id_type=MESH)
+
+    def center(i, carry):
+        rows = pl.ds(pl.multiple_of(i * 16, 16), 16)
+        xs[mine + chip, rows, :] = (
+            resid_ref[rows, :].astype(jnp.float32) - dbias_ref[...]
+        ).astype(jnp.bfloat16)
+        return carry
+
+    lax.fori_loop(0, BLK // 16, center, 0)
+    pl.semaphore_wait(barrier, len(greeted))
+
+    sent = []
+
+    def push(src, dst, send, recv, who):
+        copy = pltpu.make_async_remote_copy(
+            src_ref=src, dst_ref=dst, send_sem=send, recv_sem=recv,
+            device_id=who, device_id_type=MESH,
+        )
+        copy.start()
+        sent.append(copy)
+        return copy
+
+    def share(n, slot, part_of, who):
+        where = xs.at[slot] if part_of is None else xs.at[slot, pl.ds(part_of * half, half), :]
+        return push(where, where, ag_send.at[n], ag_recv.at[n], who)
+
+    here = mine + chip
+    a1 = share(1, here, 0, by_x)
+    a3 = share(3, here, 1, by_y)
+    a2 = share(2, here, 1, by_x)
+    a4 = share(4, here, 0, by_y)
+    a0 = share(0, here, None, sibling)
+
+    ids = ids_ref[...]
+    first_block = (t * n_z + z) * BLK_DEV
+    for b in range(BLK_DEV):
+        hit = jnp.max(jnp.where(ids == first_block + b, 1.0, 0.0), axis=1, keepdims=True)
+        active[:, b * BLK:(b + 1) * BLK] = jnp.broadcast_to(hit, (hit.shape[0], BLK))
+
+    def encode(group, chip_of):
+        slot = group + chip_of
+        row_block = chip_of * 2 + group // chips
+
+        def tile(n, carry):
+            cols = pl.ds(pl.multiple_of(n * 256, 256), 256)
+            pre = jnp.dot(xs[slot], enc_v[:, cols], preferred_element_type=jnp.float32)
+            pre = jnp.maximum(pre + ebias_ref[:, cols], 0.0)
+            on = active[pl.ds(row_block, 1), cols]
+            codes[slot, :, cols] = jnp.where(on > 0.0, pre, 0.0).astype(jnp.bfloat16)
+            return carry
+
+        lax.fori_loop(0, enc_v.shape[1] // 256, tile, 0)
+
+    load_enc.wait()
+    encode(mine, chip)
+    a0.wait_recv()
+    encode(other, chip)
+    a1.wait_recv()
+    a5 = share(5, mine + chip_x, 0, by_y)
+    a3.wait_recv()
+    a6 = share(6, mine + chip_y, 1, by_x)
+    a2.wait_recv()
+    a7 = share(7, mine + chip_x, None, sibling)
+    a4.wait_recv()
+    a8 = share(8, mine + chip_y, None, sibling)
+    encode(mine, chip_x)
+    encode(mine, chip_y)
+    a7.wait_recv()
+    encode(other, chip_x)
+    a8.wait_recv()
+    encode(other, chip_y)
+    a5.wait_recv()
+    a9 = share(9, mine + chip_d, 0, sibling)
+    a6.wait_recv()
+    a10 = share(10, mine + chip_d, 1, sibling)
+    load_dec.wait()
+    encode(mine, chip_d)
+    a9.wait_recv()
+    a10.wait_recv()
+    encode(other, chip_d)
+
+    def decode(k, group):
+        def tile(n, carry):
+            cols = pl.ds(pl.multiple_of(n * own + k * step, step), step)
+            value = jnp.dot(
+                codes[pl.ds(group, chips)].reshape(chips * BLK, codes.shape[2]),
+                dec_v[:, cols], preferred_element_type=jnp.float32,
+            )
+            to = pl.ds(pl.multiple_of(n * step, step), step)
+            part[k, pl.ds(group, chips), :, to] = value.astype(jnp.bfloat16).reshape(
+                chips, BLK, step
+            )
+            return carry
+
+        lax.fori_loop(0, n_z, tile, 0)
+
+    def add(k, slot, more):
+        part[k, slot] = (
+            part[k, slot].astype(jnp.float32) + more.astype(jnp.float32)
+        ).astype(jnp.bfloat16)
+
+    def places(k):
+        if k % 2 == 0:
+            return x, y, by_x, by_y, lambda a, b: b * 2 + a
+        return y, x, by_y, by_x, lambda a, b: a * 2 + b
+
+    core_copy, first_copy, second_copy, z_copy = {}, {}, {}, {}
+
+    def make(k):
+        decode(k, other)
+        core_copy[k] = push(
+            part.at[k, pl.ds(other, chips)], from_core.at[k],
+            core_send.at[k], core_recv.at[k], sibling,
+        )
+        decode(k, mine)
+
+    def over_core(k):
+        a, b, by_a, by_b, at = places(k)
+        core_copy[k].wait_recv()
+        for i in range(2):
+            away = at(1 - a, i)
+            add(k, mine + away, from_core[k, away])
+            first_copy[k, i] = push(
+                part.at[k, mine + away], from_first.at[k, i],
+                first_send.at[k, i], first_recv.at[k, i], by_a,
+            )
+        for i in range(2):
+            kept = at(a, i)
+            add(k, mine + kept, from_core[k, kept])
+
+    def over_first(k):
+        a, b, by_a, by_b, at = places(k)
+        for i in range(2):
+            first_copy[k, i].wait_recv()
+        add(k, mine + at(a, 1 - b), from_first[k, 1 - b])
+        second_copy[k] = push(
+            part.at[k, mine + at(a, 1 - b)], from_second.at[k],
+            second_send.at[k], second_recv.at[k], by_b,
+        )
+        add(k, mine + chip, from_first[k, b])
+
+    def over_second(k):
+        second_copy[k].wait_recv()
+        add(k, mine + chip, from_second[k])
+        for d in range(1, n_z):
+            cols = pl.ds(pl.multiple_of(along_z[d - 1][1] * step, step), step)
+            z_copy[k, d] = push(
+                part.at[k, mine + chip, :, cols], from_z.at[k, d - 1],
+                z_send.at[k, d - 1], z_recv.at[k, d - 1], along_z[d - 1],
+            )
+
+    def over_z(k):
+        for d in range(1, n_z):
+            z_copy[k, d].wait_recv()
+        cols = pl.ds(pl.multiple_of(z * step, step), step)
+        total = part[k, mine + chip, :, cols].astype(jnp.float32)
+        for d in range(1, n_z):
+            total = total + from_z[k, d - 1].astype(jnp.float32)
+        there = pl.ds(pl.multiple_of(z * own + k * step, step), step)
+        out_ref[:, k * step:(k + 1) * step] = (
+            total + dbias_ref[:, there] - resid_ref[:, there].astype(jnp.float32)
+        )
+
+    for k in range(CHUNKS):
+        make(k)
+        if k >= 1:
+            over_core(k - 1)
+    over_core(CHUNKS - 1)
+    for k in range(CHUNKS):
+        over_first(k)
+        if k >= 1:
+            over_second(k - 1)
+    over_second(CHUNKS - 1)
+    for k in range(CHUNKS):
+        over_z(k)
+    for copy in sent:
+        copy.wait_send()
+
+
+def fused_local(resid, enc_weight, enc_bias, dec_weight, dec_bias, active_ids):
+    n_t, n_z = lax.axis_size("tok"), lax.axis_size("feat")
+    rows, width = resid.shape
+    feats = enc_weight.shape[1]
+    own = width // n_z
+    step = own // CHUNKS
+    chips = n_t // 2
+    vmem = pl.BlockSpec(memory_space=pltpu.VMEM)
+    hbm = pl.BlockSpec(memory_space=pl.ANY)
+    dma = pltpu.SemaphoreType.DMA
+    wide = n_z * step
+    return pl.pallas_call(
+        fused,
+        out_shape=jax.ShapeDtypeStruct((rows, own), jnp.float32),
+        in_specs=[vmem, hbm, vmem, hbm, vmem, vmem],
+        out_specs=vmem,
+        scratch_shapes=[
+            pltpu.VMEM((n_t, BLK, width), jnp.bfloat16),
+            pltpu.VMEM((width, feats), jnp.bfloat16),
+            pltpu.VMEM((feats, width), jnp.bfloat16),
+            pltpu.VMEM((n_t, BLK, feats), jnp.bfloat16),
+            pltpu.VMEM((CHUNKS, n_t, BLK, wide), jnp.bfloat16),
+            pltpu.VMEM((CHUNKS, chips, BLK, wide), jnp.bfloat16),
+            pltpu.VMEM((CHUNKS, 2, BLK, wide), jnp.bfloat16),
+            pltpu.VMEM((CHUNKS, BLK, wide), jnp.bfloat16),
+            pltpu.VMEM((CHUNKS, n_z - 1, BLK, step), jnp.bfloat16),
+            pltpu.VMEM((n_t, feats), jnp.float32),
+            dma((2,)), dma((11,)), dma((11,)),
+            dma((CHUNKS,)), dma((CHUNKS,)), dma((CHUNKS, 2)), dma((CHUNKS, 2)),
+            dma((CHUNKS,)), dma((CHUNKS,)), dma((CHUNKS, n_z - 1)), dma((CHUNKS, n_z - 1)),
+        ],
+        compiler_params=pltpu.CompilerParams(
+            collective_id=1, has_side_effects=True, vmem_limit_bytes=60 * 1024 * 1024
+        ),
+        cost_estimate=pl.CostEstimate(
+            flops=4 * n_t * BLK * feats * width, bytes_accessed=4 * feats * width,
+            transcendentals=0,
+        ),
+    )(resid, enc_weight, enc_bias[None, :], dec_weight, dec_bias[None, :], active_ids)
+
+
 def solution(mesh):
     in_specs = (
         P("tok", None),
@@ -78,4 +334,5 @@
         P(),
     )
     out_specs = P("tok", "feat")
-    return jax.shard_map(local, mesh=mesh, in_specs=in_specs, out_specs=out_specs, check_vma=False)
+    body = fused_local if mesh.shape["tok"] == 8 else local
+    return jax.shard_map(body, mesh=mesh, in_specs=in_specs, out_specs=out_specs, check_vma=False)

time: 669 us -> 114 us (0.17)
  matrix products: 346 us -> 0 us
  waiting for transfers between devices: 245 us -> 0 us
  Pallas kernels: 0 us -> 112 us
  local copies, waits for them, and re-layouts: 48.4 us -> 1.89 us
  other arithmetic: 14.4 us -> 0 us
  between operations: 13.1 us -> 0.01 us
    dot_general x32 -> x0, matrix products: 346 us -> none  [the longest x8 235 us: one_block(): jnp.einsum('rs,sbd->rbd', select, contrib.reshape(slot_count, BLK, width)...]
    reduce_scatter x2 -> x0, waiting for transfers between devices: 189 us -> none  [the longest x1 145 us: local(): lax.psum_scatter(rounded.astype(jnp.bfloat16), 'feat', scatter_dimension=...]
    pallas_call x0 -> x1, Pallas kernels: none -> 112 us  [fused_local(): pl.pallas_call(fused, out_shape=jax.ShapeDtypeStruct((rows, own), jnp.flo...]
    all_gather x1 -> x0, waiting for transfers between devices: 56 us -> none  [local(): gathered = lax.all_gather(centered, 'tok', axis=0, tiled=True)]
    convert_element_type x8 -> x0, local copies, waits for them, and re-layouts: 18.4 us -> none  [one_block(): picked = picked.astype(jnp.bfloat16).reshape(slot_count * BLK, width)]
    convert_element_type x4 -> x0, other arithmetic: 11.4 us -> none  [the longest x1 9.01 us: local(): partial_value.astype(jnp.bfloat16)]
    optimization_barrier x1 -> x0, local copies, waits for them, and re-layouts: 11.2 us -> none  [local(): lax.optimization_barrier(partial_value.astype(jnp.bfloat16))]
    unnamed x1, local copies, waits for them, and re-layouts: 11.2 us -> 1.89 us
  transfers between devices with their start and end apart: 3 -> 0, of which waited for: 3 -> 0; matrix products, arithmetic and copies ran while one was open for 0% -> 0% of each run, Pallas kernels for 0% -> 0%
where the time goes in v1:
time: 114 us
  Pallas kernels  112 us (98%)
  local copies, waits for them, and re-layouts  1.89 us (2%)
    pallas_call x1, Pallas kernels, fused_local(): pl.pallas_call(fused, out_shape=jax.ShapeDtypeStruct((rows, own), jnp.flo...  112 us

profile of v1, /device:TPU:0, one launch (start us, length us, event | category | flops | bytes accessed | tf_op | source)
XLA Modules:
  0.0 113.6 jit_solution(7414737383307079048)
XLA Ops:
  0.0 111.7 %shard_map.64 = f32[128,1024]{1,0:T(8,128)} custom-call(bf16[128,4096]{1,0:T(8,128)(2,1)} %resid_ref.1, bf16[4096,1024]{1,0:T(8,128)(2,1)} %enc_ref.1, f32[1,1024]{1,0:T(1,128)} %bitcast.3, bf16[1024,4096]{1,0:T(8,128)(2,1)} %dec_ref.1, f32[1,4096]{1,0:T(1,128)} %bitcast.2, s32[8,96]{1,0:T(8,128)} %ids_ref.1), custom_call_target="tpu_custom_call" | custom-call | flops 17179869184 | bytes 16777216 | tf_op jit(solution)/shard_map/pallas_call | solution.py:297
  111.7 1.9 %copy.8 = f32[128,1024]{1,0:T(8,128)} copy(f32[128,1024]{1,0:T(8,128)} %shard_map.64) | data formatting | bytes 1048576

commit v2 on v1

--- a/solution.py
+++ b/solution.py
@@ -7,7 +7,9 @@
 
 BLK = 128
 BLK_DEV = 8
-CHUNKS = 4
+CHUNKS = 8
+LEFT = 48
+WIDE = BLK - LEFT
 MESH = pl.DeviceIdType.MESH
 
 
@@ -73,7 +75,7 @@
 
 
 def fused(resid_ref, enc_ref, ebias_ref, dec_ref, dbias_ref, ids_ref, out_ref,
-          xs, enc_v, dec_v, codes, part, from_core, from_first, from_second, from_z, active,
+          xs, late, enc_v, dec_v, codes, part, from_core, from_first, from_second, from_z, active,
           load_sem, ag_send, ag_recv, core_send, core_recv, first_send, first_recv,
           second_send, second_recv, z_send, z_recv):
     t = lax.axis_index("tok")
@@ -126,16 +128,34 @@
         sent.append(copy)
         return copy
 
-    def share(n, slot, part_of, who):
-        where = xs.at[slot] if part_of is None else xs.at[slot, pl.ds(part_of * half, half), :]
-        return push(where, where, ag_send.at[n], ag_recv.at[n], who)
-
+    def share(n, src, dst, who):
+        return push(src, dst, ag_send.at[n], ag_recv.at[n], who)
+
+    def rows_of(slot, start, count):
+        return xs.at[slot, pl.ds(pl.multiple_of(start, 16), count), :]
+
+    def late_rows(start, count):
+        return late.at[core, pl.ds(pl.multiple_of(start, 16), count), :]
+
+    qx = lax.rem(z, 2)
+    qy = 1 - qx
+    beside = (t, z + 1 - 2 * qx)
     here = mine + chip
-    a1 = share(1, here, 0, by_x)
-    a3 = share(3, here, 1, by_y)
-    a2 = share(2, here, 1, by_x)
-    a4 = share(4, here, 0, by_y)
-    a0 = share(0, here, None, sibling)
+    end = BLK - LEFT
+
+    def start_row(n, q, who):
+        where = rows_of(here, q * end, LEFT)
+        return share(n, where, where, who)
+
+    def middle(n, who):
+        where = rows_of(here, LEFT, BLK - 2 * LEFT)
+        return share(n, where, where, who)
+
+    a1 = start_row(1, qx, by_x)
+    a3 = start_row(3, qy, by_y)
+    a2 = middle(2, by_x)
+    a4 = middle(4, by_y)
+    a0 = share(0, xs.at[here], xs.at[here], sibling)
 
     ids = ids_ref[...]
     first_block = (t * n_z + z) * BLK_DEV
@@ -143,59 +163,81 @@
         hit = jnp.max(jnp.where(ids == first_block + b, 1.0, 0.0), axis=1, keepdims=True)
         active[:, b * BLK:(b + 1) * BLK] = jnp.broadcast_to(hit, (hit.shape[0], BLK))
 
-    def encode(group, chip_of):
-        slot = group + chip_of
-        row_block = chip_of * 2 + group // chips
-
+    def encode(rows, takes):
         def tile(n, carry):
             cols = pl.ds(pl.multiple_of(n * 256, 256), 256)
-            pre = jnp.dot(xs[slot], enc_v[:, cols], preferred_element_type=jnp.float32)
+            pre = jnp.dot(rows[...], enc_v[:, cols], preferred_element_type=jnp.float32)
             pre = jnp.maximum(pre + ebias_ref[:, cols], 0.0)
-            on = active[pl.ds(row_block, 1), cols]
-            codes[slot, :, cols] = jnp.where(on > 0.0, pre, 0.0).astype(jnp.bfloat16)
+            for group, chip_of, to, at, count in takes:
+                on = active[pl.ds(chip_of * 2 + group // chips, 1), cols]
+                codes[group + chip_of, pl.ds(to, count), cols] = jnp.where(
+                    on > 0.0, pre[at:at + count], 0.0
+                ).astype(jnp.bfloat16)
             return carry
 
         lax.fori_loop(0, enc_v.shape[1] // 256, tile, 0)
 
+    def encode_wide(group, chip_of, q):
+        first = pl.multiple_of(q * LEFT, 16)
+        encode(rows_of(group + chip_of, first, WIDE), [(group, chip_of, first, 0, WIDE)])
+
+    def encode_late(group):
+        encode(late.at[group // chips], [
+            (group, chip_x, pl.multiple_of((1 - qx) * end, 16), 0, LEFT),
+            (group, chip_y, pl.multiple_of((1 - qy) * end, 16), LEFT, LEFT),
+            (group, chip_d, 0, 2 * LEFT, BLK),
+        ])
+
     load_enc.wait()
-    encode(mine, chip)
+    encode(xs.at[here], [(mine, chip, 0, 0, BLK)])
+    a1.wait_recv()
+    a5 = share(5, rows_of(mine + chip_x, qx * end, LEFT), late_rows(0, LEFT), beside)
+    a3.wait_recv()
+    a6 = share(6, rows_of(mine + chip_y, qy * end, LEFT), late_rows(LEFT, LEFT), beside)
+    a2.wait_recv()
+    a7 = share(7, rows_of(mine + chip_x, qx * half, half), late_rows(2 * LEFT + qx * half, half), by_y)
+    wide_x = rows_of(mine + chip_x, qx * LEFT, WIDE)
+    a9 = share(9, wide_x, wide_x, sibling)
+    a4.wait_recv()
+    a8 = share(8, rows_of(mine + chip_y, qy * half, half), late_rows(2 * LEFT + qy * half, half), by_x)
+    wide_y = rows_of(mine + chip_y, qy * LEFT, WIDE)
+    a10 = share(10, wide_y, wide_y, sibling)
     a0.wait_recv()
-    encode(other, chip)
-    a1.wait_recv()
-    a5 = share(5, mine + chip_x, 0, by_y)
-    a3.wait_recv()
-    a6 = share(6, mine + chip_y, 1, by_x)
-    a2.wait_recv()
-    a7 = share(7, mine + chip_x, None, sibling)
-    a4.wait_recv()
-    a8 = share(8, mine + chip_y, None, sibling)
-    encode(mine, chip_x)
-    encode(mine, chip_y)
+    encode(xs.at[other + chip], [(other, chip, 0, 0, BLK)])
+    encode_wide(mine, chip_x, qx)
+    encode_wide(mine, chip_y, qy)
+    a9.wait_recv()
+    encode_wide(other, chip_x, qx)
+    a10.wait_recv()
+    encode_wide(other, chip_y, qy)
+    a5.wait_recv()
+    a11 = share(11, late_rows(0, LEFT), late_rows(0, LEFT), sibling)
+    a6.wait_recv()
+    a12 = share(12, late_rows(LEFT, LEFT), late_rows(LEFT, LEFT), sibling)
     a7.wait_recv()
-    encode(other, chip_x)
+    where = late_rows(2 * LEFT + qx * half, half)
+    a13 = share(13, where, where, sibling)
     a8.wait_recv()
-    encode(other, chip_y)
-    a5.wait_recv()
-    a9 = share(9, mine + chip_d, 0, sibling)
-    a6.wait_recv()
-    a10 = share(10, mine + chip_d, 1, sibling)
+    where = late_rows(2 * LEFT + qy * half, half)
+    a14 = share(14, where, where, sibling)
+    encode_late(mine)
     load_dec.wait()
-    encode(mine, chip_d)
-    a9.wait_recv()
-    a10.wait_recv()
-    encode(other, chip_d)
+    a11.wait_recv()
+    a12.wait_recv()
+    a13.wait_recv()
+    a14.wait_recv()
+    encode_late(other)
 
     def decode(k, group):
         def tile(n, carry):
-            cols = pl.ds(pl.multiple_of(n * own + k * step, step), step)
+            cols = pl.ds(pl.multiple_of(n * own + k * step, 2 * step), 2 * step)
             value = jnp.dot(
                 codes[pl.ds(group, chips)].reshape(chips * BLK, codes.shape[2]),
                 dec_v[:, cols], preferred_element_type=jnp.float32,
-            )
+            ).astype(jnp.bfloat16).reshape(chips, BLK, 2 * step)
             to = pl.ds(pl.multiple_of(n * step, step), step)
-            part[k, pl.ds(group, chips), :, to] = value.astype(jnp.bfloat16).reshape(
-                chips, BLK, step
-            )
+            part[k, pl.ds(group, chips), :, to] = value[:, :, :step]
+            part[k + 1, pl.ds(group, chips), :, to] = value[:, :, step:]
             return carry
 
         lax.fori_loop(0, n_z, tile, 0)
@@ -212,13 +254,14 @@
 
     core_copy, first_copy, second_copy, z_copy = {}, {}, {}, {}
 
-    def make(k):
-        decode(k, other)
-        core_copy[k] = push(
-            part.at[k, pl.ds(other, chips)], from_core.at[k],
-            core_send.at[k], core_recv.at[k], sibling,
-        )
-        decode(k, mine)
+    def make(j):
+        decode(2 * j, other)
+        for k in (2 * j, 2 * j + 1):
+            core_copy[k] = push(
+                part.at[k, pl.ds(other, chips)], from_core.at[k],
+                core_send.at[k], core_recv.at[k], sibling,
+            )
+        decode(2 * j, mine)
 
     def over_core(k):
         a, b, by_a, by_b, at = places(k)
@@ -267,16 +310,23 @@
             total + dbias_ref[:, there] - resid_ref[:, there].astype(jnp.float32)
         )
 
-    for k in range(CHUNKS):
-        make(k)
-        if k >= 1:
-            over_core(k - 1)
-    over_core(CHUNKS - 1)
-    for k in range(CHUNKS):
-        over_first(k)
-        if k >= 1:
-            over_second(k - 1)
-    over_second(CHUNKS - 1)
+    def both(stage, j):
+        if 0 <= j < pairs:
+            stage(2 * j)
+            stage(2 * j + 1)
+
+    pairs = CHUNKS // 2
+    make(0)
+    make(1)
+    both(over_core, 0)
+    for j in range(2, pairs):
+        make(j)
+        both(over_core, j - 1) if j == 2 else None
+    for j in range(pairs):
+        both(over_first, j)
+        both(over_core, j + 2)
+        both(over_second, j - 1)
+    both(over_second, pairs - 1)
     for k in range(CHUNKS):
         over_z(k)
     for copy in sent:
@@ -301,6 +351,7 @@
         out_specs=vmem,
         scratch_shapes=[
             pltpu.VMEM((n_t, BLK, width), jnp.bfloat16),
+            pltpu.VMEM((2, 2 * LEFT + BLK, width), jnp.bfloat16),
             pltpu.VMEM((width, feats), jnp.bfloat16),
             pltpu.VMEM((feats, width), jnp.bfloat16),
             pltpu.VMEM((n_t, BLK, feats), jnp.bfloat16),
@@ -310,7 +361,7 @@
             pltpu.VMEM((CHUNKS, BLK, wide), jnp.bfloat16),
             pltpu.VMEM((CHUNKS, n_z - 1, BLK, step), jnp.bfloat16),
             pltpu.VMEM((n_t, feats), jnp.float32),
-            dma((2,)), dma((11,)), dma((11,)),
+            dma((2,)), dma((15,)), dma((15,)),
             dma((CHUNKS,)), dma((CHUNKS,)), dma((CHUNKS, 2)), dma((CHUNKS, 2)),
             dma((CHUNKS,)), dma((CHUNKS,)), dma((CHUNKS, n_z - 1)), dma((CHUNKS, n_z - 1)),
         ],

time: 114 us -> 97.9 us (0.86)
  Pallas kernels: 112 us -> 95.8 us
    pallas_call x1, Pallas kernels: 112 us -> 95.8 us  [fused_local(): pl.pallas_call(fused, out_shape=jax.ShapeDtypeStruct((rows, own), jnp.flo...]
where the time goes in v2:
time: 97.9 us; the launch traced here: 97.7 us
  Pallas kernels  95.8 us (98%)
  local copies, waits for them, and re-layouts  1.89 us (2%)
    pallas_call x1, Pallas kernels, fused_local(): pl.pallas_call(fused, out_shape=jax.ShapeDtypeStruct((rows, own), jnp.flo...  95.8 us

profile of v2, /device:TPU:0, one launch (start us, length us, event | category | flops | bytes accessed | tf_op | source)
XLA Modules:
  0.0 97.7 jit_solution(2130920147956441819)
XLA Ops:
  0.0 95.8 %shard_map.64 = f32[128,1024]{1,0:T(8,128)} custom-call(bf16[128,4096]{1,0:T(8,128)(2,1)} %resid_ref.1, bf16[4096,1024]{1,0:T(8,128)(2,1)} %enc_ref.1, f32[1,1024]{1,0:T(1,128)} %bitcast.3, bf16[1024,4096]{1,0:T(8,128)(2,1)} %dec_ref.1, f32[1,4096]{1,0:T(1,128)} %bitcast.2, s32[8,96]{1,0:T(8,128)} %ids_ref.1), custom_call_target="tpu_custom_call" | custom-call | flops 17179869184 | bytes 16777216 | tf_op jit(solution)/shard_map/pallas_call | solution.py:347
  95.8 1.9 %copy.8 = f32[128,1024]{1,0:T(8,128)} copy(f32[128,1024]{1,0:T(8,128)} %shard_map.64) | data formatting | bytes 1048576

commit v3 on v2

--- a/solution.py
+++ b/solution.py
@@ -317,18 +317,22 @@
 
     pairs = CHUNKS // 2
     make(0)
+    both(over_core, 0)
     make(1)
-    both(over_core, 0)
-    for j in range(2, pairs):
+    both(over_core, 1)
+    make(2)
+    both(over_first, 0)
+    both(over_core, 2)
+    for j in range(3, pairs):
         make(j)
-        both(over_core, j - 1) if j == 2 else None
-    for j in range(pairs):
+    for j in range(1, pairs):
         both(over_first, j)
         both(over_core, j + 2)
         both(over_second, j - 1)
+        both(over_z, j - 2)
     both(over_second, pairs - 1)
-    for k in range(CHUNKS):
-        over_z(k)
+    both(over_z, pairs - 2)
+    both(over_z, pairs - 1)
     for copy in sent:
         copy.wait_send()
 

time: 97.9 us -> 94.1 us (0.961)
  Pallas kernels: 95.8 us -> 92.1 us
    pallas_call x1, Pallas kernels: 95.8 us -> 92.1 us  [fused_local(): pl.pallas_call(fused, out_shape=jax.ShapeDtypeStruct((rows, own), jnp.flo...]
where the time goes in v3:
time: 94.1 us; the launch traced here: 94 us
  Pallas kernels  92.1 us (98%)
  local copies, waits for them, and re-layouts  1.89 us (2%)
    pallas_call x1, Pallas kernels, fused_local(): pl.pallas_call(fused, out_shape=jax.ShapeDtypeStruct((rows, own), jnp.flo...  92.1 us
    unnamed x1, local copies, waits for them, and re-layouts  1.89 us

profile of v3, /device:TPU:0, one launch (start us, length us, event | category | flops | bytes accessed | tf_op | source)
XLA Modules:
  0.0 94.0 jit_solution(5299234175412322566)
XLA Ops:
  0.0 92.1 %shard_map.64 = f32[128,1024]{1,0:T(8,128)} custom-call(bf16[128,4096]{1,0:T(8,128)(2,1)} %resid_ref.1, bf16[4096,1024]{1,0:T(8,128)(2,1)} %enc_ref.1, f32[1,1024]{1,0:T(1,128)} %bitcast.3, bf16[1024,4096]{1,0:T(8,128)(2,1)} %dec_ref.1, f32[1,4096]{1,0:T(1,128)} %bitcast.2, s32[8,96]{1,0:T(8,128)} %ids_ref.1), custom_call_target="tpu_custom_call" | custom-call | flops 17179869184 | bytes 16777216 | tf_op jit(solution)/shard_map/pallas_call | solution.py:351
  92.1 1.9 %copy.8 = f32[128,1024]{1,0:T(8,128)} copy(f32[128,1024]{1,0:T(8,128)} %shard_map.64) | data formatting | bytes 1048576
